TPU v7x, 512 devices: a whole 4x8x8 slice. The times are simulated.
512 devices in a mesh: gx: 64 (over z_lo, x, y), gy: 8 (over z_hi, core).
Axes of the slice: x: 4, y: 8, z: 8 (z_hi: 4, z_lo: 2; z = z_hi * 2 + z_lo), core: 2. Of those that a mesh axis runs over, the one named last changes fastest.
Arguments:
- position: float32 [3, 2097152], P(None, ('gx', 'gy')), may hold values from 0.05 to 0.95, as said below
- momentum: float32 [3, 2097152], P(None, ('gx', 'gy')), may hold values from -1.6 to 1.6, as said below
- cell_first: int32 [3, 2097152], P(None, ('gx', 'gy')), may hold values from 0 to 255, as said below
- cell_second: int32 [3, 2097152], P(None, ('gx', 'gy')), may hold values from 0 to 255, as said below
- destination: int32 [2097152], P(('gx', 'gy')), may hold values from 0 to 4, as said below
- slot_index: int32 [2097152], P(('gx', 'gy')), may hold values from 0 to 4095, as said below
- pull_position: float32 [3, 2097152], P(None, ('gx', 'gy')), may hold values from -6 to 6
- pull_momentum: float32 [3, 2097152], P(None, ('gx', 'gy')), may hold values from -6 to 6
Outputs:
- grad_position: float32 [3, 2097152], P(None, ('gx', 'gy'))
- grad_momentum: float32 [3, 2097152], P(None, ('gx', 'gy'))
Inputs may be any that keep to these rules, and one draw needn't show every extreme that they name: `destination`: 0: the particle stays on its device; 1 and 2: it moves to the next and to the previous device along gx; 3 and 4: to the next and to the previous device along gy (both axes wrap). From the particles of one device at most 256 go to each of its four neighbours, and in every draw some device sends exactly 256 to one neighbour. Between two neighbouring devices as many particles move one way as the other. A particle that moves to the next (previous) device along an axis lies in the last (first) cell layer of its device along that axis in cell_first. Over all particles the destination device and slot_index fill every index of every device exactly once. `cell_first`: the first component is below 2, the second below 8, the third below 256. `cell_second`: the cell_first of the particle that lands at this index, moved with it: a particle moving along gx goes from the last layer to the first or from the first to the last, likewise along gy; other components stay. The first component is below 2, the second below 8, the third below 256. `position`: A particle's drift_one leaves its cell along an axis exactly where destination sends it across that axis, in that direction. `momentum`: momenta of particles that move carry them across the cell face toward their destination.
All inputs are finite; a program needn't handle non-finite values.
Results may differ from a plain program's by a relative error of at most 0.000058.
Values sent between devices are 32-bit elements; how exact they have to be, the bound alone decides.
No kernel may reach another device: no remote copies, remote signals or barrier semaphores. Data moves between devices by JAX's collectives and lax.ppermute only.
A program may use at most 64 MiB of HBM per device.

v0:
```python
import jax
import jax.numpy as jnp
from jax import lax
from jax.sharding import PartitionSpec as P

CX = 2
CY = 8
NZ = 256
MOVE_MOST = 256
highest = lax.Precision.HIGHEST
step_size = 0.25
strength = 0.02


def with_halo(x, sides, width):
    for axis, dim in sides:
        peers, length = (lax.axis_size(axis), x.shape[dim])
        up = [(i, (i + 1) % peers) for i in range(peers)]
        down = [(j, i) for i, j in up]
        last = lax.slice_in_dim(x, length - width, length, axis=dim)
        first = lax.slice_in_dim(x, 0, width, axis=dim)
        before = lax.ppermute(last, axis, up)
        after = lax.ppermute(first, axis, down)
        x = jnp.concatenate([before, x, after], axis=dim)
    return x


def kernel_block(targets, sources, extent, reach_cells):
    distance = jnp.abs(targets[:, None] - sources[None, :])
    distance = jnp.minimum(distance, extent - distance)
    return jnp.exp(-distance.astype(jnp.float32) / reach_cells)


def cloud_weights(cell_block, frac_block, plane_count, row_count, depth_cells):
    index_row = jnp.arange(row_count, dtype=jnp.int32)[:, None]
    corner = (cell_block[1] * plane_count + cell_block[0])[None, :]
    hit_base = (index_row == corner).astype(jnp.float32)
    hit_east = (index_row == corner + 1).astype(jnp.float32)
    hit_north = (index_row == corner + plane_count).astype(jnp.float32)
    hit_both = (index_row == corner + plane_count + 1).astype(jnp.float32)
    west_weight = (1.0 - frac_block[0])[None, :]
    east_weight = frac_block[0][None, :]
    south_weight = (1.0 - frac_block[1])[None, :]
    north_weight = frac_block[1][None, :]
    planar = (
        hit_base * (west_weight * south_weight)
        + hit_east * (east_weight * south_weight)
        + hit_north * (west_weight * north_weight)
        + hit_both * (east_weight * north_weight)
    )
    slope_east = (hit_east - hit_base) * south_weight + (hit_both - hit_north) * north_weight
    slope_north = (hit_north - hit_base) * west_weight + (hit_both - hit_east) * east_weight
    index_depth = jnp.arange(depth_cells, dtype=jnp.int32)[:, None]
    lower_hit = (index_depth == cell_block[2][None, :]).astype(jnp.float32)
    upper_hit = (index_depth == ((cell_block[2] + 1) % depth_cells)[None, :]).astype(jnp.float32)
    vertical = lower_hit * (1.0 - frac_block[2])[None, :] + upper_hit * frac_block[2][None, :]
    slope_up = upper_hit - lower_hit
    return (planar, slope_east, slope_north, vertical, slope_up)


def particle_blocks(values):
    particle_count = values.shape[1]
    block_width = min(512, particle_count)
    return values.reshape(values.shape[0], particle_count // block_width, block_width).transpose(
        1, 0, 2
    )


def deposit(scales, cell_ids, offsets):
    layers = scales.shape[0]
    row_count = (CY + 1) * (CX + 1)

    def add_block(running, pieces):
        cell_block, frac_block, scale_block = pieces
        weights = cloud_weights(cell_block, frac_block, CX + 1, row_count, NZ)
        spread = scale_block[:, None, :] * weights[0][None]
        return (running + jnp.einsum("crb,zb->crz", spread, weights[3], precision=highest), None)

    initial = jnp.zeros((layers, row_count, NZ), jnp.float32)
    running, unused = lax.scan(
        add_block,
        initial,
        (particle_blocks(cell_ids), particle_blocks(offsets), particle_blocks(scales)),
    )
    return running.reshape(layers, CY + 1, CX + 1, NZ)


def sample_fields(fields, cell_ids, offsets, slopes):
    layers = fields.shape[0]
    row_count = fields.shape[1] * fields.shape[2]
    flattened = fields.reshape(layers * row_count, NZ)

    def one_block(pieces):
        cell_block, frac_block = pieces
        block_width = cell_block.shape[1]
        weights = cloud_weights(cell_block, frac_block, fields.shape[2], row_count, NZ)
        columns = jnp.concatenate([weights[3], weights[4]], 1) if slopes else weights[3]
        contracted = jnp.dot(
            flattened, columns, precision=highest, preferred_element_type=jnp.float32
        )
        contracted = contracted.reshape(layers, row_count, -1)
        nearby = contracted[:, :, :block_width]
        results = [jnp.sum(nearby * weights[0][None], axis=1)]
        if slopes:
            results.append(jnp.sum(nearby * weights[1][None], axis=1))
            results.append(jnp.sum(nearby * weights[2][None], axis=1))
            results.append(jnp.sum(contracted[:, :, block_width:] * weights[0][None], axis=1))
        return jnp.stack(results, 0)

    blocked = lax.map(one_block, (particle_blocks(cell_ids), particle_blocks(offsets)))
    return blocked.transpose(1, 2, 0, 3).reshape(blocked.shape[1], layers, cell_ids.shape[1])


def fold_planes(slab):
    planes = slab.shape[2]
    widened = with_halo(slab, (("gx", 2),), 2)
    return jnp.concatenate(
        [
            widened[:, :, 0:1],
            widened[:, :, 1:2] + widened[:, :, 2:3],
            widened[:, :, 3 : planes + 1],
            widened[:, :, planes + 1 : planes + 2] + widened[:, :, planes + 2 : planes + 3],
            widened[:, :, planes + 3 : planes + 4],
        ],
        axis=2,
    )


def smooth_depth(field):
    depth_cells = field.shape[-1]
    axis_cells = jnp.arange(depth_cells, dtype=jnp.int32)
    matrix = kernel_block(axis_cells, axis_cells, depth_cells, depth_cells / 16.0)
    return jnp.dot(
        field.reshape(-1, depth_cells),
        matrix,
        precision=highest,
        preferred_element_type=jnp.float32,
    ).reshape(field.shape)


def sum_lines(field):
    members = lax.axis_size("gy")
    band_rows = field.shape[1]
    own_rows = band_rows - 1
    extent = own_rows * members
    reach_cells = extent / 4.0
    anchor = lax.axis_index("gy") * own_rows
    targets = (anchor + jnp.arange(-1, own_rows + 2, dtype=jnp.int32)) % extent
    initial = jnp.zeros((field.shape[0], own_rows + 3, field.shape[2], field.shape[3]), jnp.float32)
    gathered = lax.all_gather(field, "gy", axis=1, tiled=True)
    length = gathered.shape[1]
    positions = jnp.arange(length, dtype=jnp.int32)
    sources = (positions // band_rows * own_rows + positions % band_rows) % extent
    weights = kernel_block(targets, sources, extent, reach_cells)
    return initial + jnp.einsum("ab,cbxz->caxz", weights, gathered, precision=highest)


def force_field(density):
    potential = sum_lines(smooth_depth(fold_planes(density)))
    potential = strength * potential
    centre = potential[:, 1:-1, 1:-1]
    push_east = -0.5 * (potential[:, 1:-1, 2:] - potential[:, 1:-1, :-2])
    push_north = -0.5 * (potential[:, 2:, 1:-1] - potential[:, :-2, 1:-1])
    push_up = -0.5 * (jnp.roll(centre, -1, 3) - jnp.roll(centre, 1, 3))
    return jnp.concatenate([push_east, push_north, push_up], 0)


def force_pullback(pushes, cell_ids, offsets, pull_force):
    folded = fold_planes(deposit(pull_force, cell_ids, offsets))
    across = 0.5 * (folded[0:1, :, 2:] - folded[0:1, :, :-2])
    upward = folded[2:3, :, 1:-1]
    across = across + 0.5 * (jnp.roll(upward, -1, 3) - jnp.roll(upward, 1, 3))
    line_sums = sum_lines(jnp.concatenate([across, folded[1:2, :, 1:-1]], 0))
    summed = line_sums[0:1, 1:-1] + 0.5 * (line_sums[1:2, 2:] - line_sums[1:2, :-2])
    density_pull = strength * smooth_depth(summed)
    sampled = sample_fields(jnp.concatenate([pushes, density_pull], 0), cell_ids, offsets, True)
    slopes = sampled[1:]
    return jnp.sum(slopes[:, :3] * pull_force[None], axis=1) + slopes[:, 3]


def pack_moves(destination, capacity):
    particle_count = destination.shape[0]
    grouped = jnp.argsort(destination, stable=True)
    group_size = jnp.sum(
        (destination[None, :] == jnp.arange(5, dtype=jnp.int32)[:, None]).astype(jnp.int32), axis=1
    )
    earlier = jnp.arange(5, dtype=jnp.int32)[None, :] < jnp.arange(5, dtype=jnp.int32)[:, None]
    opening = jnp.sum(jnp.where(earlier, group_size[None, :], 0), axis=1)
    lane_index = jnp.arange(capacity, dtype=jnp.int32)
    chosen = jnp.stack(
        [
            grouped[jnp.minimum(opening[move_code] + lane_index, particle_count - 1)]
            for move_code in range(1, 5)
        ],
        0,
    )
    filled = lane_index[None, :] < group_size[1:5, None]
    return (chosen, filled)


def trade_pairs(outward_x, outward_y):
    widened_x = with_halo(outward_x, (("gx", 1),), 1)
    widened_y = with_halo(outward_y, (("gy", 1),), 1)
    return (widened_x[:, 0], widened_x[:, 3], widened_y[:, 0], widened_y[:, 3])


def local(
    position,
    momentum,
    cell_first,
    cell_second,
    destination,
    slot_index,
    pull_position,
    pull_momentum,
):
    particle_count = position.shape[1]
    unit_mass = jnp.ones((1, particle_count), jnp.float32)
    drift_one = position + step_size * momentum
    push_one = force_field(deposit(unit_mass, cell_first, drift_one))
    kick_one = momentum + step_size * sample_fields(push_one, cell_first, drift_one, False)[0]
    eastward = (destination == 1).astype(jnp.float32) - (destination == 2).astype(jnp.float32)
    northward = (destination == 3).astype(jnp.float32) - (destination == 4).astype(jnp.float32)
    shift_cells = jnp.stack([eastward, northward, jnp.zeros_like(eastward)], 0)
    payload = jnp.concatenate([drift_one - shift_cells, kick_one], 0)
    chosen, filled = pack_moves(destination, MOVE_MOST)
    slot_marks = jnp.where(filled, slot_index[chosen], particle_count).astype(jnp.float32)
    parcel = jnp.where(filled[None], payload[:, chosen], 0.0)
    parcel = jnp.concatenate([parcel, slot_marks[None]], 0)
    arrivals = trade_pairs(
        jnp.stack([parcel[:, 1], parcel[:, 0]], 1), jnp.stack([parcel[:, 3], parcel[:, 2]], 1)
    )
    arrivals = jnp.concatenate(arrivals, 1)
    received = arrivals[6].astype(jnp.int32)
    staying = jnp.where(destination == 0, slot_index, particle_count)
    placed = jnp.concatenate([staying, received], 0)
    arrived = (
        jnp.zeros((6, particle_count), jnp.float32)
        .at[:, placed]
        .set(jnp.concatenate([payload, arrivals[:6]], 1), mode="drop")
    )
    drift_two = arrived[:3] + step_size * arrived[3:]
    push_two = force_field(deposit(unit_mass, cell_second, drift_two))
    grad_drift_two = pull_position + force_pullback(
        push_two, cell_second, drift_two, step_size * pull_momentum
    )
    grad_kick_two = pull_momentum + step_size * grad_drift_two
    returning = jnp.concatenate([grad_drift_two, grad_kick_two], 0)
    sent_back = jnp.where(
        received[None] < particle_count,
        returning[:, jnp.minimum(received, particle_count - 1)],
        0.0,
    )
    sent_back = sent_back.reshape(6, 4, MOVE_MOST)
    homecoming = trade_pairs(sent_back[:, 0:2], sent_back[:, 2:4])
    returned = jnp.stack([homecoming[1], homecoming[0], homecoming[3], homecoming[2]], 1)
    gathered_home = jnp.where(destination[None] == 0, returning[:, slot_index], 0.0)
    home_spots = jnp.where(filled, chosen, particle_count).reshape(-1)
    gathered_home = gathered_home.at[:, home_spots].set(returned.reshape(6, -1), mode="drop")
    grad_drift_one = gathered_home[:3] + force_pullback(
        push_one, cell_first, drift_one, step_size * gathered_home[3:]
    )
    grad_momentum = gathered_home[3:] + step_size * grad_drift_one
    return (grad_drift_one, grad_momentum)


def solution(mesh):
    return jax.shard_map(
        local,
        mesh=mesh,
        in_specs=(
            P(None, ("gx", "gy")),
            P(None, ("gx", "gy")),
            P(None, ("gx", "gy")),
            P(None, ("gx", "gy")),
            P(("gx", "gy")),
            P(("gx", "gy")),
            P(None, ("gx", "gy")),
            P(None, ("gx", "gy")),
        ),
        out_specs=(P(None, ("gx", "gy")), P(None, ("gx", "gy"))),
        check_vma=False,
    )
```

profile of v0, /device:TPU:1, one launch (start us, length us, event | category | flops | bytes accessed | tf_op | source)
XLA Modules:
  0.0 329.2 jit_solution(8306297615378816670)
XLA Ops:
  1.4 1.0 maximum_subtract_fusion
  2.4 12.2 %while.91 = (s32[]{:T(128)}, f32[1,27,256]{2,1,0:T(8,128)S(1)}, s32[8,3,512]{2,1,0:T(4,128)}, f32[8,3,512]{2,1,0:T(4,128)S(1)}, s32[]{:T(128)}, /*index=5*/s32[]{:T(128)}, s32[]{}, s32[]{}) while((s32[]{:T(128)}, f32[1,27,256]{2,1,0:T(8,128)S(1)}, s32[8,3,512]{2,1,0:T(4,128)}, f32[8,3,512]{2,1,0:T(4,128)S(1)}, s32[]{:T(128)}, ...), condition=%wide.region_2.3_spmd.clone, body=%wide.region_1.2_spmd.clone.sunk | while | flops 43300868 | bytes 131215 | solution.py:80
  2.5 0.8 dynamic-slice_add_fusion.17
  4.0 0.8 dynamic-slice_add_fusion.17
  5.5 0.8 dynamic-slice_add_fusion.17
  7.0 0.8 dynamic-slice_add_fusion.17
  8.5 0.8 dynamic-slice_add_fusion.17
  10.1 0.8 dynamic-slice_add_fusion.17
  11.6 0.8 dynamic-slice_add_fusion.17
  13.1 0.8 dynamic-slice_add_fusion.17
  14.7 4.0 %collective-permute-start = (f32[1,9,2,256]{3,1,2,0:T(8,128)S(1)}, f32[1,9,2,256]{3,1,2,0:T(8,128)S(1)}, u32[]{:S(2)}, u32[]{:S(2)}) collective-permute-start(f32[1,9,2,256]{3,1,2,0:T(8,128)S(1)} %copy.330), channel_id=1, source_target_pairs={{0,8},{8,16},{16,24},{24,32},{32,40},{40,48},{48,56},{56,64},{64,7... | collective-permute-start | bytes 55304 | tf_op jit(solution)/shard_map/ppermute | solution.py:22
  18.7 7.8 %collective-permute-start.1 = (f32[1,9,2,256]{3,1,2,0:T(8,128)S(1)}, f32[1,9,2,256]{3,1,2,0:T(8,128)S(1)}, u32[]{:S(2)}, u32[]{:S(2)}) collective-permute-start(f32[1,9,2,256]{3,1,2,0:T(8,128)S(1)} %copy.334), channel_id=1, source_target_pairs={{8,0},{16,8},{24,16},{32,24},{40,32},{48,40},{56,48},{64,56},{72,6... | collective-permute-start | bytes 55304 | tf_op jit(solution)/shard_map/ppermute | solution.py:23
  28.8 5.8 %sort.17 = (s32[4096]{0:T(1024)}, s32[4096]{0:T(1024)S(1)}) sort(s32[4096]{0:T(1024)S(1)} %copy-done.3, s32[4096]{0:T(1024)S(1)} %iota.435), dimensions={0}, to_apply=%region_6.7 | sort | flops 49152 | bytes 65536 | tf_op jit(solution)/shard_map/jit(argsort)/sort | solution.py:183
  34.6 1.7 gather_fusion
  36.4 1.7 gather_fusion.1
  39.4 1.7 gather_fusion.2
  41.1 1.7 gather_fusion.3
  43.0 6.2 %gather_fusion.5 = s32[1024]{0:T(1024)S(1)} fusion(s32[4096]{0:T(1024)S(1)} %copy-done, s32[1024]{0:T(1024)S(1)} %broadcast_clamp_fusion.1), kind=kCustom, calls=%fused_computation.5 | custom fusion | bytes 12288 | tf_op jit(solution)/shard_map/gather | solution.py:227
  49.8 20.6 %all-gather = f32[72,5,256]{2,1,0:T(8,128)S(1)} all-gather(f32[9,5,256]{2,1,0:T(8,128)S(1)} %fusion.143), channel_id=2, replica_groups=mesh['gx'=64,'gy'=8] {'gy'}, dimensions={0}, use_global_device_ids=true | all-gather | bytes 414720 | tf_op jit(solution)/shard_map/all_gather | solution.py:150
  71.3 12.9 %while.88 = (s32[]{:T(128)}, f32[8,1,3,512]{3,2,1,0:T(4,128)S(1)}, s32[8,3,512]{2,1,0:T(4,128)}, f32[8,3,512]{2,1,0:T(4,128)S(1)}, f32[81,256]{1,0:T(8,128)S(1)}, /*index=5*/s32[]{:T(128)}, s32[]{:T(128)}, s32[]{}, s32[]{}) while((s32[]{:T(128)}, f32[8,1,3,512]{3,2,1,0:T(4,128)S(1)}, s32[8,3,512]{2,1,0:T(4,128)}, f32[8,3,512]{2,1,0:T(4,128)S(1)}, ...), condition=%wide.region_5.6_spmd, body=%wide.region_3.5_spmd.sunk | while | flops 128303104 | bytes 955537 | solution.py:110
  71.3 0.8 dynamic-slice_add_fusion.14
  74.6 0.8 dynamic-slice_add_fusion.14
  76.2 0.8 dynamic-slice_add_fusion.14
  79.4 0.8 dynamic-slice_add_fusion.14
  85.0 2.8 gather_fusion.4
  88.0 2.1 collective-permute-start.5
  90.1 4.4 %collective-permute-start.4 = (f32[7,1,256]{2,1,0:T(1,128)S(1)}, f32[7,1,256]{2,1,0:T(1,128)S(1)}, u32[]{:S(2)}, u32[]{:S(2)}) collective-permute-start(f32[7,1,256]{2,1,0:T(1,128)S(1)} %get-tuple-element.759), channel_id=1, source_target_pairs={{0,1},{1,2},{2,3},{3,4},{4,5},{5,6},{6,7},{7,0},{8,9},{9,10},{10,1... | collective-permute-start | bytes 21512 | tf_op jit(solution)/shard_map/ppermute | solution.py:22
  94.5 4.4 %collective-permute-start.3 = (f32[7,1,256]{2,1,0:T(1,128)S(1)}, f32[7,1,256]{2,1,0:T(1,128)S(1)}, u32[]{:S(2)}, u32[]{:S(2)}) collective-permute-start(f32[7,1,256]{2,1,0:T(1,128)S(1)} %get-tuple-element.757), channel_id=1, source_target_pairs={{8,0},{16,8},{24,16},{32,24},{40,32},{48,40},{56,48},{64,56},{72,6... | collective-permute-start | bytes 21512 | tf_op jit(solution)/shard_map/ppermute | solution.py:23
  98.9 1.9 collective-permute-start.2
  100.9 6.6 %collective-permute-done.2 = f32[7,1,256]{2,1,0:T(1,128)S(1)} collective-permute-done((f32[7,1,256]{2,1,0:T(1,128)S(1)}, f32[7,1,256]{2,1,0:T(1,128)S(1)}, u32[]{:S(2)}, u32[]{:S(2)}) %collective-permute-start.2) | collective-permute-done | bytes 7200 | tf_op jit(solution)/shard_map/ppermute | solution.py:22
  107.6 2.2 copy.281
  109.9 14.1 %scatter_custom_fusion = f32[6,4096]{0,1:T(8,128)S(1)} fusion(s32[5120]{0:T(1024)S(1)} %bitcast.436, f32[5120,6]{1,0:T(8,128)} %copy.281, f32[]{:T(128)} %constant.568.clone.1), kind=kCustom, calls=%fused_computation.335 | custom fusion | bytes 98816 | tf_op jit(solution)/shard_map/scatter | solution.py:240
  123.9 2.6 fusion.253
  126.6 2.4 copy.335
  129.6 12.2 %while.92 = (s32[]{:T(128)}, f32[1,27,256]{2,1,0:T(8,128)S(1)}, s32[8,3,512]{2,1,0:T(4,128)}, f32[8,3,512]{2,1,0:T(4,128)S(1)}, s32[]{:T(128)}, /*index=5*/s32[]{:T(128)}, s32[]{}, s32[]{}) while((s32[]{:T(128)}, f32[1,27,256]{2,1,0:T(8,128)S(1)}, s32[8,3,512]{2,1,0:T(4,128)}, f32[8,3,512]{2,1,0:T(4,128)S(1)}, s32[]{:T(128)}, ...), condition=%wide.region_10.11_spmd.clone, body=%wide.region_9.10_spmd.clone.sunk | while | flops 43300868 | bytes 131215 | solution.py:80
  129.7 0.8 dynamic-slice_add_fusion.18
  131.2 0.8 dynamic-slice_add_fusion.18
  132.7 0.8 dynamic-slice_add_fusion.18
  134.2 0.8 dynamic-slice_add_fusion.18
  141.9 13.4 %while.93 = (s32[]{:T(128)}, f32[3,27,256]{2,1,0:T(8,128)S(1)}, f32[8,3,512]{2,1,0:T(4,128)S(1)}, s32[8,3,512]{2,1,0:T(4,128)}, f32[8,3,512]{2,1,0:T(4,128)S(1)}, /*index=5*/s32[]{:T(128)}, s32[]{:T(128)}, s32[]{}, s32[]{}) while((s32[]{:T(128)}, f32[3,27,256]{2,1,0:T(8,128)S(1)}, f32[8,3,512]{2,1,0:T(4,128)S(1)}, ...), condition=%wide.region_12.13_spmd.clone, body=%wide.region_11.12_spmd.clone.sunk | while | flops 128304640 | bytes 370843 | solution.py:80
  155.4 1.9 collective-permute-start.6
  157.4 7.6 %collective-permute-start.7 = (f32[1,9,2,256]{3,1,2,0:T(8,128)S(1)}, f32[1,9,2,256]{3,1,2,0:T(8,128)S(1)}, u32[]{:S(2)}, u32[]{:S(2)}) collective-permute-start(f32[1,9,2,256]{3,1,2,0:T(8,128)S(1)} %copy.341), channel_id=1, source_target_pairs={{8,0},{16,8},{24,16},{32,24},{40,32},{48,40},{56,48},{64,56},{72,6... | collective-permute-start | bytes 55304 | tf_op jit(solution)/shard_map/ppermute | solution.py:23
  165.0 1.9 collective-permute-start.9
  166.9 7.6 %collective-permute-start.8 = (f32[3,9,2,256]{3,1,2,0:T(8,128)S(1)}, f32[3,9,2,256]{3,1,2,0:T(8,128)S(1)}, u32[]{:S(2)}, u32[]{:S(2)}) collective-permute-start(f32[3,9,2,256]{3,1,2,0:T(8,128)S(1)} %copy.344), channel_id=1, source_target_pairs={{8,0},{16,8},{24,16},{32,24},{40,32},{48,40},{56,48},{64,56},{72,6... | collective-permute-start | bytes 165896 | tf_op jit(solution)/shard_map/ppermute | solution.py:23
  175.0 18.5 %all-gather.1 = f32[72,5,256]{2,1,0:T(8,128)S(1)} all-gather(f32[9,5,256]{2,1,0:T(8,128)S(1)} %fusion.141), channel_id=3, replica_groups=mesh['gx'=64,'gy'=8] {'gy'}, dimensions={0}, use_global_device_ids=true | all-gather | bytes 414720 | tf_op jit(solution)/shard_map/all_gather | solution.py:150
  194.5 14.8 %all_gather.14 = f32[2,72,3,256]{3,0,2,1:T(2,128)S(1)} all-gather(f32[2,9,3,256]{3,0,2,1:T(2,128)S(1)} %copy.298), channel_id=1, replica_groups=mesh['gx'=64,'gy'=8] {'gy'}, dimensions={1}, use_global_device_ids=true | all-gather | bytes 497664 | tf_op jit(solution)/shard_map/all_gather | solution.py:150
  210.3 16.8 %while.89 = (s32[]{:T(128)}, f32[8,4,4,512]{3,2,1,0:T(4,128)S(1)}, s32[8,3,512]{2,1,0:T(4,128)}, f32[8,3,512]{2,1,0:T(4,128)S(1)}, f32[108,256]{1,0:T(8,128)S(1)}, /*index=5*/s32[]{:T(128)}, s32[]{:T(128)}, s32[]{}, s32[]{}) while((s32[]{:T(128)}, f32[8,4,4,512]{3,2,1,0:T(4,128)S(1)}, s32[8,3,512]{2,1,0:T(4,128)}, ...), condition=%wide.region_18.19_spmd, body=%wide.region_13.18_spmd.sunk | while | flops 341865984 | bytes 4495505 | solution.py:110
  228.1 2.8 gather_fusion.7
  231.2 2.2 collective-permute-start.10
  233.4 3.1 collective-permute-start.11
  236.5 2.6 collective-permute-start.12
  239.1 3.8 %collective-permute-start.13 = (f32[6,1,256]{2,1,0:T(1,128)S(1)}, f32[6,1,256]{2,1,0:T(1,128)S(1)}, u32[]{:S(2)}, u32[]{:S(2)}) collective-permute-start(f32[6,1,256]{2,1,0:T(1,128)S(1)} %get-tuple-element.771), channel_id=1, source_target_pairs={{0,1},{1,2},{2,3},{3,4},{4,5},{5,6},{6,7},{7,0},{8,9},{9,10},{10,1... | collective-permute-start | bytes 18440 | tf_op jit(solution)/shard_map/ppermute | solution.py:22
  243.0 14.1 %gather_fusion.6 = f32[4096,6]{1,0:T(8,128)} fusion(f32[6,4096]{0,1:T(8,128)S(1)} %copy.303, s32[4096]{0:T(1024)S(1)} %get-tuple-element.774), kind=kCustom, calls=%fused_computation.6 | custom fusion | bytes 212992 | tf_op jit(solution)/shard_map/gather | solution.py:257
  257.0 3.6 %select_bitcast_fusion = f32[6,4096]{0,1:T(8,128)S(1)} fusion(f32[4096,6]{1,0:T(8,128)} %gather_fusion.6, pred[4096]{0:T(1024)(128)(4,1)S(1)} %get-tuple-element.613), kind=kLoop, calls=%fused_computation.324 | loop fusion | flops 24576 | bytes 200704 | tf_op jit(solution)/shard_map/jit(_where)/select_n | solution.py:257
  260.9 4.1 %scatter_fusion = f32[6,4096]{0,1:T(8,128)S(1)} fusion(f32[6,4096]{0,1:T(8,128)S(1)} %select_bitcast_fusion, s32[1024]{0:T(1024)S(1)} %bitcast.437, f32[1024,6]{1,0:T(8,128)S(1)} %bitcast.352), kind=kCustom, calls=%fused_computation.9 | custom fusion | bytes 77824 | tf_op jit(solution)/shard_map/scatter | solution.py:259
  265.0 2.7 fusion.252
  267.7 2.2 copy.349
  270.0 13.4 %while.94 = (s32[]{:T(128)}, f32[3,27,256]{2,1,0:T(8,128)S(1)}, f32[8,3,512]{2,1,0:T(4,128)S(1)}, s32[8,3,512]{2,1,0:T(4,128)}, f32[8,3,512]{2,1,0:T(4,128)S(1)}, /*index=5*/s32[]{:T(128)}, s32[]{:T(128)}, s32[]{}, s32[]{}) while((s32[]{:T(128)}, f32[3,27,256]{2,1,0:T(8,128)S(1)}, f32[8,3,512]{2,1,0:T(4,128)S(1)}, ...), condition=%wide.region_22.23_spmd.clone, body=%wide.region_21.22_spmd.clone.sunk | while | flops 128304640 | bytes 370843 | solution.py:80
  270.0 0.9 dynamic-slice_add_fusion.20
  283.5 1.9 collective-permute-start.15
  285.5 7.6 %collective-permute-start.14 = (f32[3,9,2,256]{3,1,2,0:T(8,128)S(1)}, f32[3,9,2,256]{3,1,2,0:T(8,128)S(1)}, u32[]{:S(2)}, u32[]{:S(2)}) collective-permute-start(f32[3,9,2,256]{3,1,2,0:T(8,128)S(1)} %copy.352), channel_id=1, source_target_pairs={{8,0},{16,8},{24,16},{32,24},{40,32},{48,40},{56,48},{64,56},{72,6... | collective-permute-start | bytes 165896 | tf_op jit(solution)/shard_map/ppermute | solution.py:23
  294.2 1.2 collective-permute-done.14
  295.7 14.8 %all_gather.15 = f32[2,72,3,256]{3,0,2,1:T(2,128)S(1)} all-gather(f32[2,9,3,256]{3,0,2,1:T(2,128)S(1)} %copy.315), channel_id=1, replica_groups=mesh['gx'=64,'gy'=8] {'gy'}, dimensions={1}, use_global_device_ids=true | all-gather | bytes 497664 | tf_op jit(solution)/shard_map/all_gather | solution.py:150
  311.4 16.8 %while.90 = (s32[]{:T(128)}, f32[8,4,4,512]{3,2,1,0:T(4,128)S(1)}, s32[8,3,512]{2,1,0:T(4,128)}, f32[8,3,512]{2,1,0:T(4,128)S(1)}, f32[108,256]{1,0:T(8,128)S(1)}, /*index=5*/s32[]{:T(128)}, s32[]{:T(128)}, s32[]{}, s32[]{}) while((s32[]{:T(128)}, f32[8,4,4,512]{3,2,1,0:T(4,128)S(1)}, s32[8,3,512]{2,1,0:T(4,128)}, ...), condition=%wide.region_28.29_spmd, body=%wide.region_23.28_spmd.sunk | while | flops 341865984 | bytes 4495505 | solution.py:110
  (657 shorter events, 94.8 us)
Async XLA Ops:
  2.4 24.2 %copy-start.3 = (s32[4096]{0:T(1024)S(1)}, s32[4096]{0:T(1024)}, u32[]{:S(2)}) copy-start(s32[4096]{0:T(1024)} %param.26) | copy-start | bytes 49156
  14.7 34.7 %collective-permute-start = (f32[1,9,2,256]{3,1,2,0:T(8,128)S(1)}, f32[1,9,2,256]{3,1,2,0:T(8,128)S(1)}, u32[]{:S(2)}, u32[]{:S(2)}) collective-permute-start(f32[1,9,2,256]{3,1,2,0:T(8,128)S(1)} %copy.330), channel_id=1, source_target_pairs={{0,8},{8,16},{16,24},{24,32},{32,40},{40,48},{48,56},{56,64},{64,7... | collective-permute-start | bytes 55304 | tf_op jit(solution)/shard_map/ppermute | solution.py:22
  18.7 30.7 %collective-permute-start.1 = (f32[1,9,2,256]{3,1,2,0:T(8,128)S(1)}, f32[1,9,2,256]{3,1,2,0:T(8,128)S(1)}, u32[]{:S(2)}, u32[]{:S(2)}) collective-permute-start(f32[1,9,2,256]{3,1,2,0:T(8,128)S(1)} %copy.334), channel_id=1, source_target_pairs={{8,0},{16,8},{24,16},{32,24},{40,32},{48,40},{56,48},{64,56},{72,6... | collective-permute-start | bytes 55304 | tf_op jit(solution)/shard_map/ppermute | solution.py:23
  34.6 8.3 %copy-start = (s32[4096]{0:T(1024)S(1)}, s32[4096]{0:T(1024)}, u32[]{:S(2)}) copy-start(s32[4096]{0:T(1024)} %param.27) | copy-start | bytes 49156
  43.0 6.3 %copy-start.5 = (f32[3,4096]{1,0:T(4,128)S(1)}, f32[3,4096]{1,0:T(4,128)}, u32[]{:S(2)}) copy-start(f32[3,4096]{1,0:T(4,128)} %param.29) | copy-start | bytes 147460
  71.3 13.0 %copy-start.4 = (f32[3,4096]{1,0:T(4,128)S(1)}, f32[3,4096]{1,0:T(4,128)}, u32[]{:S(2)}) copy-start(f32[3,4096]{1,0:T(4,128)} %param.23) | copy-start | bytes 147460
  88.0 12.8 %collective-permute-start.5 = (f32[7,1,256]{2,1,0:T(1,128)S(1)}, f32[7,1,256]{2,1,0:T(1,128)S(1)}, u32[]{:S(2)}, u32[]{:S(2)}) collective-permute-start(f32[7,1,256]{2,1,0:T(1,128)S(1)} %get-tuple-element.758), channel_id=1, source_target_pairs={{1,0},{2,1},{3,2},{4,3},{5,4},{6,5},{7,6},{0,7},{9,8},{10,9},{11,1... | collective-permute-start | bytes 21512 | tf_op jit(solution)/shard_map/ppermute | solution.py:23
  90.1 10.8 %collective-permute-start.4 = (f32[7,1,256]{2,1,0:T(1,128)S(1)}, f32[7,1,256]{2,1,0:T(1,128)S(1)}, u32[]{:S(2)}, u32[]{:S(2)}) collective-permute-start(f32[7,1,256]{2,1,0:T(1,128)S(1)} %get-tuple-element.759), channel_id=1, source_target_pairs={{0,1},{1,2},{2,3},{3,4},{4,5},{5,6},{6,7},{7,0},{8,9},{9,10},{10,1... | collective-permute-start | bytes 21512 | tf_op jit(solution)/shard_map/ppermute | solution.py:22
  94.5 6.4 %collective-permute-start.3 = (f32[7,1,256]{2,1,0:T(1,128)S(1)}, f32[7,1,256]{2,1,0:T(1,128)S(1)}, u32[]{:S(2)}, u32[]{:S(2)}) collective-permute-start(f32[7,1,256]{2,1,0:T(1,128)S(1)} %get-tuple-element.757), channel_id=1, source_target_pairs={{8,0},{16,8},{24,16},{32,24},{40,32},{48,40},{56,48},{64,56},{72,6... | collective-permute-start | bytes 21512 | tf_op jit(solution)/shard_map/ppermute | solution.py:23
  98.9 8.6 %collective-permute-start.2 = (f32[7,1,256]{2,1,0:T(1,128)S(1)}, f32[7,1,256]{2,1,0:T(1,128)S(1)}, u32[]{:S(2)}, u32[]{:S(2)}) collective-permute-start(f32[7,1,256]{2,1,0:T(1,128)S(1)} %get-tuple-element.756), channel_id=1, source_target_pairs={{0,8},{8,16},{16,24},{24,32},{32,40},{40,48},{48,56},{56,64},{64,7... | collective-permute-start | bytes 21512 | tf_op jit(solution)/shard_map/ppermute | solution.py:22
  126.6 2.4 copy-start.2
  155.4 19.1 %collective-permute-start.6 = (f32[1,9,2,256]{3,1,2,0:T(8,128)S(1)}, f32[1,9,2,256]{3,1,2,0:T(8,128)S(1)}, u32[]{:S(2)}, u32[]{:S(2)}) collective-permute-start(f32[1,9,2,256]{3,1,2,0:T(8,128)S(1)} %copy.337), channel_id=1, source_target_pairs={{0,8},{8,16},{16,24},{24,32},{32,40},{40,48},{48,56},{56,64},{64,7... | collective-permute-start | bytes 55304 | tf_op jit(solution)/shard_map/ppermute | solution.py:22
  157.4 17.2 %collective-permute-start.7 = (f32[1,9,2,256]{3,1,2,0:T(8,128)S(1)}, f32[1,9,2,256]{3,1,2,0:T(8,128)S(1)}, u32[]{:S(2)}, u32[]{:S(2)}) collective-permute-start(f32[1,9,2,256]{3,1,2,0:T(8,128)S(1)} %copy.341), channel_id=1, source_target_pairs={{8,0},{16,8},{24,16},{32,24},{40,32},{48,40},{56,48},{64,56},{72,6... | collective-permute-start | bytes 55304 | tf_op jit(solution)/shard_map/ppermute | solution.py:23
  165.0 29.2 %collective-permute-start.9 = (f32[3,9,2,256]{3,1,2,0:T(8,128)S(1)}, f32[3,9,2,256]{3,1,2,0:T(8,128)S(1)}, u32[]{:S(2)}, u32[]{:S(2)}) collective-permute-start(f32[3,9,2,256]{3,1,2,0:T(8,128)S(1)} %copy.345), channel_id=1, source_target_pairs={{0,8},{8,16},{16,24},{24,32},{32,40},{40,48},{48,56},{56,64},{64,7... | collective-permute-start | bytes 165896 | tf_op jit(solution)/shard_map/ppermute | solution.py:22
  166.9 27.3 %collective-permute-start.8 = (f32[3,9,2,256]{3,1,2,0:T(8,128)S(1)}, f32[3,9,2,256]{3,1,2,0:T(8,128)S(1)}, u32[]{:S(2)}, u32[]{:S(2)}) collective-permute-start(f32[3,9,2,256]{3,1,2,0:T(8,128)S(1)} %copy.344), channel_id=1, source_target_pairs={{8,0},{16,8},{24,16},{32,24},{40,32},{48,40},{56,48},{64,56},{72,6... | collective-permute-start | bytes 165896 | tf_op jit(solution)/shard_map/ppermute | solution.py:23
  210.3 17.1 %copy-start.6 = (f32[3,4096]{1,0:T(4,128)S(1)}, f32[3,4096]{1,0:T(4,128)}, u32[]{:S(2)}) copy-start(f32[3,4096]{1,0:T(4,128)} %param.28) | copy-start | bytes 147460
  231.2 29.5 %collective-permute-start.10 = (f32[6,1,256]{2,1,0:T(1,128)S(1)}, f32[6,1,256]{2,1,0:T(1,128)S(1)}, u32[]{:S(2)}, u32[]{:S(2)}) collective-permute-start(f32[6,1,256]{2,1,0:T(1,128)S(1)} %get-tuple-element.770), channel_id=1, source_target_pairs={{8,0},{16,8},{24,16},{32,24},{40,32},{48,40},{56,48},{64,56},{72,6... | collective-permute-start | bytes 18440 | tf_op jit(solution)/shard_map/ppermute | solution.py:23
  233.4 27.3 %collective-permute-start.11 = (f32[6,1,256]{2,1,0:T(1,128)S(1)}, f32[6,1,256]{2,1,0:T(1,128)S(1)}, u32[]{:S(2)}, u32[]{:S(2)}) collective-permute-start(f32[6,1,256]{2,1,0:T(1,128)S(1)} %get-tuple-element.773), channel_id=1, source_target_pairs={{0,8},{8,16},{16,24},{24,32},{32,40},{40,48},{48,56},{56,64},{64,7... | collective-permute-start | bytes 18440 | tf_op jit(solution)/shard_map/ppermute | solution.py:22
  236.5 24.2 %collective-permute-start.12 = (f32[6,1,256]{2,1,0:T(1,128)S(1)}, f32[6,1,256]{2,1,0:T(1,128)S(1)}, u32[]{:S(2)}, u32[]{:S(2)}) collective-permute-start(f32[6,1,256]{2,1,0:T(1,128)S(1)} %get-tuple-element.772), channel_id=1, source_target_pairs={{1,0},{2,1},{3,2},{4,3},{5,4},{6,5},{7,6},{0,7},{9,8},{10,9},{11,1... | collective-permute-start | bytes 18440 | tf_op jit(solution)/shard_map/ppermute | solution.py:23
  239.1 21.6 %collective-permute-start.13 = (f32[6,1,256]{2,1,0:T(1,128)S(1)}, f32[6,1,256]{2,1,0:T(1,128)S(1)}, u32[]{:S(2)}, u32[]{:S(2)}) collective-permute-start(f32[6,1,256]{2,1,0:T(1,128)S(1)} %get-tuple-element.771), channel_id=1, source_target_pairs={{0,1},{1,2},{2,3},{3,4},{4,5},{5,6},{6,7},{7,0},{8,9},{9,10},{10,1... | collective-permute-start | bytes 18440 | tf_op jit(solution)/shard_map/ppermute | solution.py:22
  270.0 23.1 %copy-start.1 = (f32[3,4096]{0,1:T(8,128)S(1)}, f32[3,4096]{0,1:T(8,128)}, u32[]{:S(2)}) copy-start(f32[3,4096]{0,1:T(8,128)} %get-tuple-element.718) | copy-start | bytes 147460
  283.5 10.7 %collective-permute-start.15 = (f32[3,9,2,256]{3,1,2,0:T(8,128)S(1)}, f32[3,9,2,256]{3,1,2,0:T(8,128)S(1)}, u32[]{:S(2)}, u32[]{:S(2)}) collective-permute-start(f32[3,9,2,256]{3,1,2,0:T(8,128)S(1)} %copy.353), channel_id=1, source_target_pairs={{0,8},{8,16},{16,24},{24,32},{32,40},{40,48},{48,56},{56,64},{64,7... | collective-permute-start | bytes 165896 | tf_op jit(solution)/shard_map/ppermute | solution.py:22
  285.5 9.9 %collective-permute-start.14 = (f32[3,9,2,256]{3,1,2,0:T(8,128)S(1)}, f32[3,9,2,256]{3,1,2,0:T(8,128)S(1)}, u32[]{:S(2)}, u32[]{:S(2)}) collective-permute-start(f32[3,9,2,256]{3,1,2,0:T(8,128)S(1)} %copy.352), channel_id=1, source_target_pairs={{8,0},{16,8},{24,16},{32,24},{40,32},{48,40},{56,48},{64,56},{72,6... | collective-permute-start | bytes 165896 | tf_op jit(solution)/shard_map/ppermute | solution.py:23
where the time goes:
time: 334 us; the launch traced here: 329 us
  other arithmetic  71.1 us (21%)
  local copies, waits for them, and re-layouts  70.9 us (21%)
  blocking collectives  68.8 us (21%)
  starting transfers between devices  64.9 us (19%)
  matrix products  39.7 us (12%)
  waiting for transfers between devices  8.23 us (2%)
  loops' own time  3.7 us (1%)
    all_gather x4, blocking collectives, sum_lines(): gathered = lax.all_gather(field, 'gy', axis=1, tiled=True)  68.8 us
    add x56, other arithmetic, cloud_weights(): corner = (cell_block[1] * plane_count + cell_block[0])[None, :]  46.3 us
    ppermute x8, starting transfers between devices, with_halo(): after = lax.ppermute(first, axis, down)  41.8 us
    ppermute x8, starting transfers between devices, with_halo(): before = lax.ppermute(last, axis, up)  23 us
    dot_general x32, matrix products, add_block(): jnp.einsum('crb,zb->crz', spread, weights[3], precision=highest)  20.9 us
    dot_general x24, matrix products, one_block(): jnp.dot(flattened, columns, precision=highest, preferred_element_type=jnp...  15.9 us
    scatter x1, local copies, waits for them, and re-layouts, local(): arrived = jnp.zeros((6, particle_count), jnp.float32).at[:, placed].set(j...  14.1 us
    gather x1, local copies, waits for them, and re-layouts, local(): returning[:, slot_index]  14.1 us
  transfers between devices with their start and end apart: 16, of which 3 were waited for; matrix products, arithmetic and copies ran while one was open for 13% of the time, Pallas kernels for 0%

commit v1 on v0

--- a/solution.py
+++ b/solution.py
@@ -147,7 +147,8 @@
     anchor = lax.axis_index("gy") * own_rows
     targets = (anchor + jnp.arange(-1, own_rows + 2, dtype=jnp.int32)) % extent
     initial = jnp.zeros((field.shape[0], own_rows + 3, field.shape[2], field.shape[3]), jnp.float32)
-    gathered = lax.all_gather(field, "gy", axis=1, tiled=True)
+    stack = jnp.stack([field] * lax.axis_size("gy"))
+    gathered = jnp.concatenate(lax.all_to_all(stack, "gy", 0, 0), axis=1)
     length = gathered.shape[1]
     positions = jnp.arange(length, dtype=jnp.int32)
     sources = (positions // band_rows * own_rows + positions % band_rows) % extent

time: 334 us -> 349 us (1.045)
  the two profiles are of different devices: /device:TPU:1 before, /device:TPU:62 now
where the time goes in v1:
time: 349 us; the launch traced here: 344 us
  starting transfers between devices  81.7 us (23%)
  local copies, waits for them, and re-layouts  74.8 us (21%)
  waiting for transfers between devices  71.3 us (20%)
  other arithmetic  71.2 us (20%)
  matrix products  39.8 us (11%)
  loops' own time  3.7 us (1%)
    all_to_all x4, waiting for transfers between devices, sum_lines(): gathered = jnp.concatenate(lax.all_to_all(stack, 'gy', 0, 0), axis=1)  54.8 us
    add x56, other arithmetic, cloud_weights(): corner = (cell_block[1] * plane_count + cell_block[0])[None, :]  46.2 us
    ppermute x8, starting transfers between devices, with_halo(): before = lax.ppermute(last, axis, up)  43.8 us
    dot_general x32, matrix products, add_block(): jnp.einsum('crb,zb->crz', spread, weights[3], precision=highest)  20.9 us
    all_to_all x4, starting transfers between devices, sum_lines(): gathered = jnp.concatenate(lax.all_to_all(stack, 'gy', 0, 0), axis=1)  20.7 us
    ppermute x8, starting transfers between devices, with_halo(): after = lax.ppermute(first, axis, down)  17.2 us
    dot_general x24, matrix products, one_block(): jnp.dot(flattened, columns, precision=highest, preferred_element_type=jnp...  15.9 us
    ppermute x8, waiting for transfers between devices, with_halo(): after = lax.ppermute(first, axis, down)  14.2 us
  transfers between devices with their start and end apart: 20, of which 8 were waited for; matrix products, arithmetic and copies ran while one was open for 13% of the time, Pallas kernels for 0%

profile of v1, /device:TPU:62, one launch (start us, length us, event | category | flops | bytes accessed | tf_op | source)
XLA Modules:
  0.0 344.2 jit_solution(17737706330056145744)
XLA Ops:
  1.4 1.0 maximum_subtract_fusion
  2.4 12.2 %while.91 = (s32[]{:T(128)}, f32[1,27,256]{2,1,0:T(8,128)S(1)}, s32[8,3,512]{2,1,0:T(4,128)}, f32[8,3,512]{2,1,0:T(4,128)S(1)}, s32[]{:T(128)}, /*index=5*/s32[]{:T(128)}, s32[]{}, s32[]{}) while((s32[]{:T(128)}, f32[1,27,256]{2,1,0:T(8,128)S(1)}, s32[8,3,512]{2,1,0:T(4,128)}, f32[8,3,512]{2,1,0:T(4,128)S(1)}, s32[]{:T(128)}, ...), condition=%wide.region_2.3_spmd.clone, body=%wide.region_1.2_spmd.clone.sunk | while | flops 43300868 | bytes 131215 | solution.py:80
  2.5 0.8 dynamic-slice_add_fusion.17
  14.6 3.4 collective-permute-start
  18.0 2.4 collective-permute-start.1
  22.2 5.8 %sort.17 = (s32[4096]{0:T(1024)}, s32[4096]{0:T(1024)S(1)}) sort(s32[4096]{0:T(1024)S(1)} %copy-done.3, s32[4096]{0:T(1024)S(1)} %iota.435), dimensions={0}, to_apply=%region_6.7 | sort | flops 49152 | bytes 65536 | tf_op jit(solution)/shard_map/jit(argsort)/sort | solution.py:184
  28.6 1.7 gather_fusion
  30.4 1.7 gather_fusion.1
  32.8 1.7 gather_fusion.2
  35.2 1.7 gather_fusion.3
  37.0 6.2 %gather_fusion.5 = s32[1024]{0:T(1024)S(1)} fusion(s32[4096]{0:T(1024)S(1)} %copy-done, s32[1024]{0:T(1024)S(1)} %broadcast_clamp_fusion.1), kind=kCustom, calls=%fused_computation.5 | custom fusion | bytes 12288 | tf_op jit(solution)/shard_map/gather | solution.py:228
  43.9 0.9 stack.129
  44.8 10.3 %all-to-all-start = ((f32[8,1,9,5,256]{4,1,3,2,0:T(1,128)}), f32[8,1,9,5,256]{4,1,3,2,0:T(1,128)S(1)}, u32[]{:S(2)}, u32[]{:S(2)}) async-start(f32[8,1,9,5,256]{4,1,3,2,0:T(1,128)} %stack.129), calls=%async_computation | async-start | bytes 737280 | tf_op jit(solution)/shard_map/all_to_all | solution.py:151
  55.2 15.0 %all-to-all-done = f32[8,1,9,5,256]{4,1,3,2,0:T(1,128)S(1)} async-done(((f32[8,1,9,5,256]{4,1,3,2,0:T(1,128)}), f32[8,1,9,5,256]{4,1,3,2,0:T(1,128)S(1)}, u32[]{:S(2)}, u32[]{:S(2)}) %all-to-all-start) | async-done | bytes 368672 | tf_op jit(solution)/shard_map/all_to_all | solution.py:151
  71.1 13.0 %while.88 = (s32[]{:T(128)}, f32[8,1,3,512]{3,2,1,0:T(4,128)S(1)}, s32[8,3,512]{2,1,0:T(4,128)}, f32[8,3,512]{2,1,0:T(4,128)S(1)}, f32[81,256]{1,0:T(8,128)S(1)}, /*index=5*/s32[]{:T(128)}, s32[]{:T(128)}, s32[]{}, s32[]{}) while((s32[]{:T(128)}, f32[8,1,3,512]{3,2,1,0:T(4,128)S(1)}, s32[8,3,512]{2,1,0:T(4,128)}, f32[8,3,512]{2,1,0:T(4,128)S(1)}, ...), condition=%wide.region_5.6_spmd, body=%wide.region_3.5_spmd.sunk | while | flops 128303104 | bytes 955537 | solution.py:110
  74.4 0.8 dynamic-slice_add_fusion.14
  77.6 0.8 dynamic-slice_add_fusion.14
  79.2 0.8 dynamic-slice_add_fusion.14
  82.4 0.8 dynamic-slice_add_fusion.14
  84.8 2.8 gather_fusion.4
  87.8 1.9 collective-permute-start.5
  89.7 2.4 collective-permute-start.4
  92.2 3.3 collective-permute-start.3
  95.4 6.8 %collective-permute-start.2 = (f32[7,1,256]{2,1,0:T(1,128)S(1)}, f32[7,1,256]{2,1,0:T(1,128)S(1)}, u32[]{:S(2)}, u32[]{:S(2)}) collective-permute-start(f32[7,1,256]{2,1,0:T(1,128)S(1)} %get-tuple-element.766), channel_id=1, source_target_pairs={{0,8},{8,16},{16,24},{24,32},{32,40},{40,48},{48,56},{56,64},{64,7... | collective-permute-start | bytes 21512 | tf_op jit(solution)/shard_map/ppermute | solution.py:22
  102.3 1.2 collective-permute-done.2
  103.6 2.3 copy.298
  105.9 14.1 %scatter_custom_fusion = f32[6,4096]{0,1:T(8,128)S(1)} fusion(s32[5120]{0:T(1024)S(1)} %bitcast.452, f32[5120,6]{1,0:T(8,128)} %copy.298, f32[]{:T(128)} %constant.568.clone.1), kind=kCustom, calls=%fused_computation.335 | custom fusion | bytes 98816 | tf_op jit(solution)/shard_map/scatter | solution.py:241
  120.0 2.6 fusion.253
  122.6 2.4 copy.346
  125.7 13.3 %while.93 = (s32[]{:T(128)}, f32[3,27,256]{2,1,0:T(8,128)S(1)}, f32[8,3,512]{2,1,0:T(4,128)S(1)}, s32[8,3,512]{2,1,0:T(4,128)}, f32[8,3,512]{2,1,0:T(4,128)S(1)}, /*index=5*/s32[]{:T(128)}, s32[]{:T(128)}, s32[]{}, s32[]{}) while((s32[]{:T(128)}, f32[3,27,256]{2,1,0:T(8,128)S(1)}, f32[8,3,512]{2,1,0:T(4,128)S(1)}, ...), condition=%wide.region_12.13_spmd.clone, body=%wide.region_11.12_spmd.clone.sunk | while | flops 128304640 | bytes 370843 | solution.py:80
  127.4 0.8 dynamic-slice_add_fusion.19
  130.7 0.8 dynamic-slice_add_fusion.19
  139.2 12.2 %while.92 = (s32[]{:T(128)}, f32[1,27,256]{2,1,0:T(8,128)S(1)}, s32[8,3,512]{2,1,0:T(4,128)}, f32[8,3,512]{2,1,0:T(4,128)S(1)}, s32[]{:T(128)}, /*index=5*/s32[]{:T(128)}, s32[]{}, s32[]{}) while((s32[]{:T(128)}, f32[1,27,256]{2,1,0:T(8,128)S(1)}, s32[8,3,512]{2,1,0:T(4,128)}, f32[8,3,512]{2,1,0:T(4,128)S(1)}, s32[]{:T(128)}, ...), condition=%wide.region_10.11_spmd.clone, body=%wide.region_9.10_spmd.clone.sunk | while | flops 43300868 | bytes 131215 | solution.py:80
  151.4 8.4 %collective-permute-start.6 = (f32[1,9,2,256]{3,2,1,0:T(2,128)S(1)}, f32[1,9,2,256]{3,2,1,0:T(2,128)S(1)}, u32[]{:S(2)}, u32[]{:S(2)}) collective-permute-start(f32[1,9,2,256]{3,2,1,0:T(2,128)S(1)} %get-tuple-element.760), channel_id=1, source_target_pairs={{0,8},{8,16},{16,24},{24,32},{32,40},{40,48},{48,56},{56,64},{64,7... | collective-permute-start | bytes 55304 | tf_op jit(solution)/shard_map/ppermute | solution.py:22
  159.8 1.9 collective-permute-start.7
  161.8 8.1 %collective-permute-start.9 = (f32[3,9,2,256]{3,1,2,0:T(8,128)S(1)}, f32[3,9,2,256]{3,1,2,0:T(8,128)S(1)}, u32[]{:S(2)}, u32[]{:S(2)}) collective-permute-start(f32[3,9,2,256]{3,1,2,0:T(8,128)S(1)} %copy.351), channel_id=1, source_target_pairs={{0,8},{8,16},{16,24},{24,32},{32,40},{40,48},{48,56},{56,64},{64,7... | collective-permute-start | bytes 165896 | tf_op jit(solution)/shard_map/ppermute | solution.py:22
  170.0 1.9 collective-permute-start.8
  172.5 0.9 stack.135
  173.4 3.4 %all-to-all-start.1 = ((f32[8,1,9,5,256]{4,1,3,2,0:T(1,128)}), f32[8,1,9,5,256]{4,1,3,2,0:T(1,128)S(1)}, u32[]{:S(2)}, u32[]{:S(2)}) async-start(f32[8,1,9,5,256]{4,1,3,2,0:T(1,128)} %stack.135), calls=%async_computation.1 | async-start | bytes 737280 | tf_op jit(solution)/shard_map/all_to_all | solution.py:151
  176.9 3.9 %collective-permute-done.8 = f32[3,9,2,256]{3,1,2,0:T(8,128)S(1)} collective-permute-done((f32[3,9,2,256]{3,1,2,0:T(8,128)S(1)}, f32[3,9,2,256]{3,1,2,0:T(8,128)S(1)}, u32[]{:S(2)}, u32[]{:S(2)}) %collective-permute-start.8) | collective-permute-done | bytes 55328 | tf_op jit(solution)/shard_map/ppermute | solution.py:23
  181.1 10.7 %all-to-all-done.1 = f32[8,1,9,5,256]{4,1,3,2,0:T(1,128)S(1)} async-done(((f32[8,1,9,5,256]{4,1,3,2,0:T(1,128)}), f32[8,1,9,5,256]{4,1,3,2,0:T(1,128)S(1)}, u32[]{:S(2)}, u32[]{:S(2)}) %all-to-all-start.1) | async-done | bytes 368672 | tf_op jit(solution)/shard_map/all_to_all | solution.py:151
  191.8 0.9 stack.136
  192.7 3.5 %all-to-all-start.2 = ((f32[8,2,9,3,256]{4,1,3,2,0:T(2,128)}), f32[8,2,9,3,256]{4,1,3,2,0:T(2,128)S(1)}, u32[]{:S(2)}, u32[]{:S(2)}) async-start(f32[8,2,9,3,256]{4,1,3,2,0:T(2,128)} %stack.136), calls=%async_computation.2 | async-start | bytes 884736 | tf_op jit(solution)/shard_map/all_to_all | solution.py:151
  196.9 15.1 %all-to-all-done.2 = f32[8,2,9,3,256]{4,1,3,2,0:T(2,128)S(1)} async-done(((f32[8,2,9,3,256]{4,1,3,2,0:T(2,128)}), f32[8,2,9,3,256]{4,1,3,2,0:T(2,128)S(1)}, u32[]{:S(2)}, u32[]{:S(2)}) %all-to-all-start.2) | async-done | bytes 442400 | tf_op jit(solution)/shard_map/all_to_all | solution.py:151
  213.0 16.8 %while.89 = (s32[]{:T(128)}, f32[8,4,4,512]{3,2,1,0:T(4,128)S(1)}, s32[8,3,512]{2,1,0:T(4,128)}, f32[8,3,512]{2,1,0:T(4,128)S(1)}, f32[108,256]{1,0:T(8,128)S(1)}, /*index=5*/s32[]{:T(128)}, s32[]{:T(128)}, s32[]{}, s32[]{}) while((s32[]{:T(128)}, f32[8,4,4,512]{3,2,1,0:T(4,128)S(1)}, s32[8,3,512]{2,1,0:T(4,128)}, ...), condition=%wide.region_18.19_spmd, body=%wide.region_13.18_spmd.sunk | while | flops 341865984 | bytes 4495505 | solution.py:110
  230.8 2.8 gather_fusion.7
  233.9 1.9 collective-permute-start.10
  235.8 8.1 %collective-permute-start.11 = (f32[6,1,256]{2,1,0:T(1,128)S(1)}, f32[6,1,256]{2,1,0:T(1,128)S(1)}, u32[]{:S(2)}, u32[]{:S(2)}) collective-permute-start(f32[6,1,256]{2,1,0:T(1,128)S(1)} %get-tuple-element.773), channel_id=1, source_target_pairs={{0,8},{8,16},{16,24},{24,32},{32,40},{40,48},{48,56},{56,64},{64,7... | collective-permute-start | bytes 18440 | tf_op jit(solution)/shard_map/ppermute | solution.py:22
  244.0 1.9 collective-permute-start.12
  245.9 2.4 collective-permute-start.13
  248.3 14.1 %gather_fusion.6 = f32[4096,6]{1,0:T(8,128)} fusion(f32[6,4096]{0,1:T(8,128)S(1)} %copy.319, s32[4096]{0:T(1024)S(1)} %get-tuple-element.778), kind=kCustom, calls=%fused_computation.6 | custom fusion | bytes 212992 | tf_op jit(solution)/shard_map/gather | solution.py:258
  262.4 3.6 %select_bitcast_fusion = f32[6,4096]{0,1:T(8,128)S(1)} fusion(f32[4096,6]{1,0:T(8,128)} %gather_fusion.6, pred[4096]{0:T(1024)(128)(4,1)S(1)} %get-tuple-element.613), kind=kLoop, calls=%fused_computation.324 | loop fusion | flops 24576 | bytes 200704 | tf_op jit(solution)/shard_map/jit(_where)/select_n | solution.py:258
  266.3 4.1 %scatter_fusion = f32[6,4096]{0,1:T(8,128)S(1)} fusion(f32[6,4096]{0,1:T(8,128)S(1)} %select_bitcast_fusion, s32[1024]{0:T(1024)S(1)} %bitcast.453, f32[1024,6]{1,0:T(8,128)S(1)} %bitcast.368), kind=kCustom, calls=%fused_computation.9 | custom fusion | bytes 77824 | tf_op jit(solution)/shard_map/scatter | solution.py:260
  270.4 2.7 fusion.252
  273.1 2.2 copy.355
  275.3 13.4 %while.94 = (s32[]{:T(128)}, f32[3,27,256]{2,1,0:T(8,128)S(1)}, f32[8,3,512]{2,1,0:T(4,128)S(1)}, s32[8,3,512]{2,1,0:T(4,128)}, f32[8,3,512]{2,1,0:T(4,128)S(1)}, /*index=5*/s32[]{:T(128)}, s32[]{:T(128)}, s32[]{}, s32[]{}) while((s32[]{:T(128)}, f32[3,27,256]{2,1,0:T(8,128)S(1)}, f32[8,3,512]{2,1,0:T(4,128)S(1)}, ...), condition=%wide.region_22.23_spmd.clone, body=%wide.region_21.22_spmd.clone.sunk | while | flops 128304640 | bytes 370843 | solution.py:80
  288.8 4.0 %collective-permute-start.15 = (f32[3,9,2,256]{3,1,2,0:T(8,128)S(1)}, f32[3,9,2,256]{3,1,2,0:T(8,128)S(1)}, u32[]{:S(2)}, u32[]{:S(2)}) collective-permute-start(f32[3,9,2,256]{3,1,2,0:T(8,128)S(1)} %copy.359), channel_id=1, source_target_pairs={{0,8},{8,16},{16,24},{24,32},{32,40},{40,48},{48,56},{56,64},{64,7... | collective-permute-start | bytes 165896 | tf_op jit(solution)/shard_map/ppermute | solution.py:22
  293.0 1.9 collective-permute-start.14
  294.9 1.0 collective-permute-done.15
  295.9 10.3 %collective-permute-done.14 = f32[3,9,2,256]{3,1,2,0:T(8,128)S(1)} collective-permute-done((f32[3,9,2,256]{3,1,2,0:T(8,128)S(1)}, f32[3,9,2,256]{3,1,2,0:T(8,128)S(1)}, u32[]{:S(2)}, u32[]{:S(2)}) %collective-permute-start.14) | collective-permute-done | bytes 55328 | tf_op jit(solution)/shard_map/ppermute | solution.py:23
  306.5 0.9 stack.143
  307.4 3.5 %all-to-all-start.3 = ((f32[8,2,9,3,256]{4,1,3,2,0:T(2,128)}), f32[8,2,9,3,256]{4,1,3,2,0:T(2,128)S(1)}, u32[]{:S(2)}, u32[]{:S(2)}) async-start(f32[8,2,9,3,256]{4,1,3,2,0:T(2,128)} %stack.143), calls=%async_computation.3 | async-start | bytes 884736 | tf_op jit(solution)/shard_map/all_to_all | solution.py:151
  311.5 14.0 %all-to-all-done.3 = f32[8,2,9,3,256]{4,1,3,2,0:T(2,128)S(1)} async-done(((f32[8,2,9,3,256]{4,1,3,2,0:T(2,128)}), f32[8,2,9,3,256]{4,1,3,2,0:T(2,128)S(1)}, u32[]{:S(2)}, u32[]{:S(2)}) %all-to-all-start.3) | async-done | bytes 442400 | tf_op jit(solution)/shard_map/all_to_all | solution.py:151
  326.4 16.8 %while.90 = (s32[]{:T(128)}, f32[8,4,4,512]{3,2,1,0:T(4,128)S(1)}, s32[8,3,512]{2,1,0:T(4,128)}, f32[8,3,512]{2,1,0:T(4,128)S(1)}, f32[108,256]{1,0:T(8,128)S(1)}, /*index=5*/s32[]{:T(128)}, s32[]{:T(128)}, s32[]{}, s32[]{}) while((s32[]{:T(128)}, f32[8,4,4,512]{3,2,1,0:T(4,128)S(1)}, s32[8,3,512]{2,1,0:T(4,128)}, ...), condition=%wide.region_28.29_spmd, body=%wide.region_23.28_spmd.sunk | while | flops 341865984 | bytes 4495505 | solution.py:110
  (657 shorter events, 102.9 us)
Async XLA Ops:
  2.4 18.1 %copy-start.3 = (s32[4096]{0:T(1024)S(1)}, s32[4096]{0:T(1024)}, u32[]{:S(2)}) copy-start(s32[4096]{0:T(1024)} %param.26) | copy-start | bytes 49156
  14.6 28.8 %collective-permute-start = (f32[1,9,2,256]{3,2,1,0:T(2,128)S(1)}, f32[1,9,2,256]{3,2,1,0:T(2,128)S(1)}, u32[]{:S(2)}, u32[]{:S(2)}) collective-permute-start(f32[1,9,2,256]{3,2,1,0:T(2,128)S(1)} %get-tuple-element.765), channel_id=1, source_target_pairs={{0,8},{8,16},{16,24},{24,32},{32,40},{40,48},{48,56},{56,64},{64,7... | collective-permute-start | bytes 55304 | tf_op jit(solution)/shard_map/ppermute | solution.py:22
  18.0 25.4 %collective-permute-start.1 = (f32[1,9,2,256]{3,2,1,0:T(2,128)S(1)}, f32[1,9,2,256]{3,2,1,0:T(2,128)S(1)}, u32[]{:S(2)}, u32[]{:S(2)}) collective-permute-start(f32[1,9,2,256]{3,2,1,0:T(2,128)S(1)} %get-tuple-element.764), channel_id=1, source_target_pairs={{8,0},{16,8},{24,16},{32,24},{40,32},{48,40},{56,48},{64,56},{72,6... | collective-permute-start | bytes 55304 | tf_op jit(solution)/shard_map/ppermute | solution.py:23
  28.6 8.4 %copy-start = (s32[4096]{0:T(1024)S(1)}, s32[4096]{0:T(1024)}, u32[]{:S(2)}) copy-start(s32[4096]{0:T(1024)} %param.27) | copy-start | bytes 49156
  37.0 18.1 %copy-start.5 = (f32[3,4096]{1,0:T(4,128)S(1)}, f32[3,4096]{1,0:T(4,128)}, u32[]{:S(2)}) copy-start(f32[3,4096]{1,0:T(4,128)} %param.29) | copy-start | bytes 147460
  44.8 25.3 %all-to-all-start = ((f32[8,1,9,5,256]{4,1,3,2,0:T(1,128)}), f32[8,1,9,5,256]{4,1,3,2,0:T(1,128)S(1)}, u32[]{:S(2)}, u32[]{:S(2)}) async-start(f32[8,1,9,5,256]{4,1,3,2,0:T(1,128)} %stack.129), calls=%async_computation | async-start | bytes 737280 | tf_op jit(solution)/shard_map/all_to_all | solution.py:151
  71.1 13.0 %copy-start.4 = (f32[3,4096]{1,0:T(4,128)S(1)}, f32[3,4096]{1,0:T(4,128)}, u32[]{:S(2)}) copy-start(f32[3,4096]{1,0:T(4,128)} %param.23) | copy-start | bytes 147460
  87.8 14.5 %collective-permute-start.5 = (f32[7,1,256]{2,1,0:T(1,128)S(1)}, f32[7,1,256]{2,1,0:T(1,128)S(1)}, u32[]{:S(2)}, u32[]{:S(2)}) collective-permute-start(f32[7,1,256]{2,1,0:T(1,128)S(1)} %get-tuple-element.768), channel_id=1, source_target_pairs={{1,0},{2,1},{3,2},{4,3},{5,4},{6,5},{7,6},{0,7},{9,8},{10,9},{11,1... | collective-permute-start | bytes 21512 | tf_op jit(solution)/shard_map/ppermute | solution.py:23
  89.7 12.6 %collective-permute-start.4 = (f32[7,1,256]{2,1,0:T(1,128)S(1)}, f32[7,1,256]{2,1,0:T(1,128)S(1)}, u32[]{:S(2)}, u32[]{:S(2)}) collective-permute-start(f32[7,1,256]{2,1,0:T(1,128)S(1)} %get-tuple-element.769), channel_id=1, source_target_pairs={{0,1},{1,2},{2,3},{3,4},{4,5},{5,6},{6,7},{7,0},{8,9},{9,10},{10,1... | collective-permute-start | bytes 21512 | tf_op jit(solution)/shard_map/ppermute | solution.py:22
  92.2 10.2 %collective-permute-start.3 = (f32[7,1,256]{2,1,0:T(1,128)S(1)}, f32[7,1,256]{2,1,0:T(1,128)S(1)}, u32[]{:S(2)}, u32[]{:S(2)}) collective-permute-start(f32[7,1,256]{2,1,0:T(1,128)S(1)} %get-tuple-element.767), channel_id=1, source_target_pairs={{8,0},{16,8},{24,16},{32,24},{40,32},{48,40},{56,48},{64,56},{72,6... | collective-permute-start | bytes 21512 | tf_op jit(solution)/shard_map/ppermute | solution.py:23
  95.4 8.1 %collective-permute-start.2 = (f32[7,1,256]{2,1,0:T(1,128)S(1)}, f32[7,1,256]{2,1,0:T(1,128)S(1)}, u32[]{:S(2)}, u32[]{:S(2)}) collective-permute-start(f32[7,1,256]{2,1,0:T(1,128)S(1)} %get-tuple-element.766), channel_id=1, source_target_pairs={{0,8},{8,16},{16,24},{24,32},{32,40},{40,48},{48,56},{56,64},{64,7... | collective-permute-start | bytes 21512 | tf_op jit(solution)/shard_map/ppermute | solution.py:22
  122.6 2.4 copy-start.2
  151.4 20.5 %collective-permute-start.6 = (f32[1,9,2,256]{3,2,1,0:T(2,128)S(1)}, f32[1,9,2,256]{3,2,1,0:T(2,128)S(1)}, u32[]{:S(2)}, u32[]{:S(2)}) collective-permute-start(f32[1,9,2,256]{3,2,1,0:T(2,128)S(1)} %get-tuple-element.760), channel_id=1, source_target_pairs={{0,8},{8,16},{16,24},{24,32},{32,40},{40,48},{48,56},{56,64},{64,7... | collective-permute-start | bytes 55304 | tf_op jit(solution)/shard_map/ppermute | solution.py:22
  159.8 12.1 %collective-permute-start.7 = (f32[1,9,2,256]{3,2,1,0:T(2,128)S(1)}, f32[1,9,2,256]{3,2,1,0:T(2,128)S(1)}, u32[]{:S(2)}, u32[]{:S(2)}) collective-permute-start(f32[1,9,2,256]{3,2,1,0:T(2,128)S(1)} %get-tuple-element.759), channel_id=1, source_target_pairs={{8,0},{16,8},{24,16},{32,24},{40,32},{48,40},{56,48},{64,56},{72,6... | collective-permute-start | bytes 55304 | tf_op jit(solution)/shard_map/ppermute | solution.py:23
  161.8 15.1 %collective-permute-start.9 = (f32[3,9,2,256]{3,1,2,0:T(8,128)S(1)}, f32[3,9,2,256]{3,1,2,0:T(8,128)S(1)}, u32[]{:S(2)}, u32[]{:S(2)}) collective-permute-start(f32[3,9,2,256]{3,1,2,0:T(8,128)S(1)} %copy.351), channel_id=1, source_target_pairs={{0,8},{8,16},{16,24},{24,32},{32,40},{40,48},{48,56},{56,64},{64,7... | collective-permute-start | bytes 165896 | tf_op jit(solution)/shard_map/ppermute | solution.py:22
  170.0 10.8 %collective-permute-start.8 = (f32[3,9,2,256]{3,1,2,0:T(8,128)S(1)}, f32[3,9,2,256]{3,1,2,0:T(8,128)S(1)}, u32[]{:S(2)}, u32[]{:S(2)}) collective-permute-start(f32[3,9,2,256]{3,1,2,0:T(8,128)S(1)} %copy.350), channel_id=1, source_target_pairs={{8,0},{16,8},{24,16},{32,24},{40,32},{48,40},{56,48},{64,56},{72,6... | collective-permute-start | bytes 165896 | tf_op jit(solution)/shard_map/ppermute | solution.py:23
  173.4 18.4 %all-to-all-start.1 = ((f32[8,1,9,5,256]{4,1,3,2,0:T(1,128)}), f32[8,1,9,5,256]{4,1,3,2,0:T(1,128)S(1)}, u32[]{:S(2)}, u32[]{:S(2)}) async-start(f32[8,1,9,5,256]{4,1,3,2,0:T(1,128)} %stack.135), calls=%async_computation.1 | async-start | bytes 737280 | tf_op jit(solution)/shard_map/all_to_all | solution.py:151
  192.7 19.4 %all-to-all-start.2 = ((f32[8,2,9,3,256]{4,1,3,2,0:T(2,128)}), f32[8,2,9,3,256]{4,1,3,2,0:T(2,128)S(1)}, u32[]{:S(2)}, u32[]{:S(2)}) async-start(f32[8,2,9,3,256]{4,1,3,2,0:T(2,128)} %stack.136), calls=%async_computation.2 | async-start | bytes 884736 | tf_op jit(solution)/shard_map/all_to_all | solution.py:151
  213.0 17.1 %copy-start.6 = (f32[3,4096]{1,0:T(4,128)S(1)}, f32[3,4096]{1,0:T(4,128)}, u32[]{:S(2)}) copy-start(f32[3,4096]{1,0:T(4,128)} %param.28) | copy-start | bytes 147460
  233.9 32.1 %collective-permute-start.10 = (f32[6,1,256]{2,1,0:T(1,128)S(1)}, f32[6,1,256]{2,1,0:T(1,128)S(1)}, u32[]{:S(2)}, u32[]{:S(2)}) collective-permute-start(f32[6,1,256]{2,1,0:T(1,128)S(1)} %get-tuple-element.770), channel_id=1, source_target_pairs={{8,0},{16,8},{24,16},{32,24},{40,32},{48,40},{56,48},{64,56},{72,6... | collective-permute-start | bytes 18440 | tf_op jit(solution)/shard_map/ppermute | solution.py:23
  235.8 30.2 %collective-permute-start.11 = (f32[6,1,256]{2,1,0:T(1,128)S(1)}, f32[6,1,256]{2,1,0:T(1,128)S(1)}, u32[]{:S(2)}, u32[]{:S(2)}) collective-permute-start(f32[6,1,256]{2,1,0:T(1,128)S(1)} %get-tuple-element.773), channel_id=1, source_target_pairs={{0,8},{8,16},{16,24},{24,32},{32,40},{40,48},{48,56},{56,64},{64,7... | collective-permute-start | bytes 18440 | tf_op jit(solution)/shard_map/ppermute | solution.py:22
  244.0 22.1 %collective-permute-start.12 = (f32[6,1,256]{2,1,0:T(1,128)S(1)}, f32[6,1,256]{2,1,0:T(1,128)S(1)}, u32[]{:S(2)}, u32[]{:S(2)}) collective-permute-start(f32[6,1,256]{2,1,0:T(1,128)S(1)} %get-tuple-element.772), channel_id=1, source_target_pairs={{1,0},{2,1},{3,2},{4,3},{5,4},{6,5},{7,6},{0,7},{9,8},{10,9},{11,1... | collective-permute-start | bytes 18440 | tf_op jit(solution)/shard_map/ppermute | solution.py:23
  245.9 20.2 %collective-permute-start.13 = (f32[6,1,256]{2,1,0:T(1,128)S(1)}, f32[6,1,256]{2,1,0:T(1,128)S(1)}, u32[]{:S(2)}, u32[]{:S(2)}) collective-permute-start(f32[6,1,256]{2,1,0:T(1,128)S(1)} %get-tuple-element.771), channel_id=1, source_target_pairs={{0,1},{1,2},{2,3},{3,4},{4,5},{5,6},{6,7},{7,0},{8,9},{9,10},{10,1... | collective-permute-start | bytes 18440 | tf_op jit(solution)/shard_map/ppermute | solution.py:22
  288.7 22.2 %copy-start.1 = (f32[3,4096]{0,1:T(8,128)S(1)}, f32[3,4096]{0,1:T(8,128)}, u32[]{:S(2)}) copy-start(f32[3,4096]{0,1:T(8,128)} %get-tuple-element.718) | copy-start | bytes 147460
  288.8 7.1 %collective-permute-start.15 = (f32[3,9,2,256]{3,1,2,0:T(8,128)S(1)}, f32[3,9,2,256]{3,1,2,0:T(8,128)S(1)}, u32[]{:S(2)}, u32[]{:S(2)}) collective-permute-start(f32[3,9,2,256]{3,1,2,0:T(8,128)S(1)} %copy.359), channel_id=1, source_target_pairs={{0,8},{8,16},{16,24},{24,32},{32,40},{40,48},{48,56},{56,64},{64,7... | collective-permute-start | bytes 165896 | tf_op jit(solution)/shard_map/ppermute | solution.py:22
  293.0 13.2 %collective-permute-start.14 = (f32[3,9,2,256]{3,1,2,0:T(8,128)S(1)}, f32[3,9,2,256]{3,1,2,0:T(8,128)S(1)}, u32[]{:S(2)}, u32[]{:S(2)}) collective-permute-start(f32[3,9,2,256]{3,1,2,0:T(8,128)S(1)} %copy.358), channel_id=1, source_target_pairs={{8,0},{16,8},{24,16},{32,24},{40,32},{48,40},{56,48},{64,56},{72,6... | collective-permute-start | bytes 165896 | tf_op jit(solution)/shard_map/ppermute | solution.py:23
  307.4 18.1 %all-to-all-start.3 = ((f32[8,2,9,3,256]{4,1,3,2,0:T(2,128)}), f32[8,2,9,3,256]{4,1,3,2,0:T(2,128)S(1)}, u32[]{:S(2)}, u32[]{:S(2)}) async-start(f32[8,2,9,3,256]{4,1,3,2,0:T(2,128)} %stack.143), calls=%async_computation.3 | async-start | bytes 884736 | tf_op jit(solution)/shard_map/all_to_all | solution.py:151
